TPU v7x, 512 devices: a whole 4x8x8 slice. The times are simulated.
512 devices in a mesh: seq: 8 (over z), batch: 16 (over y, core), mp: 4 (over x).
Axes of the slice: x: 4, y: 8, z: 8, core: 2. Of those that a mesh axis runs over, the one named last changes fastest.
Arguments:
- queries: bfloat16 [16, 4096, 2048], P('batch', 'seq', 'mp'), may hold values from -200 to 200
- neighbour_ids: int32 [16, 64, 2], P('batch', 'seq'), may hold values from 0 to 127, as said below
- encoded: bfloat16 [128, 128, 896], P('batch'), may hold values from -6 to 6
- key_weight: bfloat16 [896, 2048], P(None, 'mp'), may hold values from -0.1875 to 0.1875
- value_weight: bfloat16 [896, 2048], P(None, 'mp'), may hold values from -0.1875 to 0.1875
Outputs:
- attended: bfloat16 [16, 4096, 2048], P('batch', 'seq', 'mp')
Inputs may be any that keep to these rules, and one draw needn't show every extreme that they name: `neighbour_ids`: the 16 neighbours named by the groups of one index of seq and batch name at most 2 neighbours held by one owner, and every such block reaches 2 for some owner.
All inputs are finite; a program needn't handle non-finite values.
Results may differ from a plain program's by a relative error of at most 0.011.
Values may be sent and summed in bfloat16 or wider, within the bound.
A program may use at most 64 MiB of HBM per device.

v0:
```python
import jax
import jax.numpy as jnp
from jax import lax
from jax.sharding import PartitionSpec as P

DH = 128


def from_behind(x, axis, by):
    devices = lax.axis_size(axis)
    pairs = [(i, i + by) for i in range(devices) if 0 <= i + by < devices]
    return lax.ppermute(x, axis, pairs)


def attend_groups(group_queries, group_keys, group_values):
    scores = jnp.einsum(
        "cqhd,ckhd->chqk", group_queries, group_keys, preferred_element_type=jnp.float32
    ) * DH ** (-0.5)
    row_max = jnp.max(scores, axis=-1, keepdims=True)
    expon = jnp.exp(scores - row_max)
    weights = (expon / jnp.sum(expon, axis=-1, keepdims=True)).astype(jnp.bfloat16)
    mixed = jnp.einsum("chqk,ckhd->cqhd", weights, group_values, preferred_element_type=jnp.float32)
    return mixed.astype(jnp.bfloat16)


def local(queries, neighbour_ids, encoded, key_weight, value_weight):
    local_queries = queries[0]
    tok_rows, width = local_queries.shape
    heads_dev = width // DH
    wanted_ids = neighbour_ids[0].reshape(-1)
    requests = wanted_ids.shape[0]
    neigh_count = neighbour_ids.shape[2]
    num_groups = requests // neigh_count
    group_len = tok_rows // num_groups
    owners = lax.axis_size("batch")
    per_owner = encoded.shape[0]
    nlen_rows = encoded.shape[1]
    enc_width = encoded.shape[2]
    capacity = max(2, requests // owners)
    owner_of = wanted_ids // per_owner
    row_of = wanted_ids % per_owner
    positions = jnp.arange(requests, dtype=jnp.int32)
    earlier = (owner_of[:, None] == owner_of[None, :]) & (positions[None, :] < positions[:, None])
    slot_rank = jnp.sum(earlier.astype(jnp.int32), axis=1)
    slot_of = owner_of * capacity + slot_rank
    places = jnp.arange(owners * capacity, dtype=jnp.int32)
    wanted_slots = jnp.sum(
        jnp.where(slot_of[:, None] == places[None, :], row_of[:, None] + 1, 0), axis=0
    )
    wanted_slots = wanted_slots.reshape(owners, capacity)
    both_weights = jnp.stack([key_weight, value_weight], axis=0)
    picked = encoded[
        jnp.maximum(
            lax.all_to_all(wanted_slots, "batch", split_axis=0, concat_axis=0, tiled=True) - 1, 0
        )
    ]
    fetched = lax.all_to_all(picked, "batch", split_axis=0, concat_axis=0, tiled=True)
    fetched = fetched.reshape(owners * capacity, nlen_rows, enc_width)[slot_of]
    projected = jnp.einsum(
        "rne,kew->krnw", fetched, both_weights, preferred_element_type=jnp.float32
    ).astype(jnp.bfloat16)
    neigh_keys = projected[0]
    neigh_values = projected[1]
    context_rows = neigh_count * nlen_rows
    group_keys = neigh_keys.reshape(num_groups, context_rows, heads_dev, DH)
    group_values = neigh_values.reshape(num_groups, context_rows, heads_dev, DH)
    last_pair = jnp.stack([group_keys[num_groups - 1], group_values[num_groups - 1]], axis=0)
    prior_pair = from_behind(last_pair, "seq", 1)
    keys_all = jnp.concatenate([prior_pair[0][None], group_keys], axis=0)
    values_all = jnp.concatenate([prior_pair[1][None], group_values], axis=0)
    padded = jnp.concatenate(
        [
            jnp.zeros((1, width), local_queries.dtype),
            local_queries,
            jnp.zeros((group_len - 1, width), local_queries.dtype),
        ],
        axis=0,
    )
    padded = padded.reshape(num_groups + 1, group_len, heads_dev, DH)
    mixed = attend_groups(padded, keys_all, values_all).reshape((num_groups + 1) * group_len, width)
    result = mixed[1 : tok_rows + 1]
    return result[None]


def solution(mesh):
    return jax.shard_map(
        local,
        mesh=mesh,
        in_specs=(
            P("batch", "seq", "mp"),
            P("batch", "seq", None),
            P("batch", None, None),
            P(None, "mp"),
            P(None, "mp"),
        ),
        out_specs=P("batch", "seq", "mp"),
        check_vma=False,
    )
```

profile of v0, /device:TPU:1, one launch (start us, length us, event | category | flops | bytes accessed | tf_op | source)
XLA Modules:
  0.0 251.5 jit_solution(6764680589072890789)
XLA Ops:
  0.0 0.0 copy-start
  0.0 0.9 copy.41
  0.9 0.1 reshape_squeeze.11
  1.0 0.2 convert_reduce_fusion
  1.2 0.1 select_reduce_fusion
  1.3 0.1 all_to_all.9
  1.4 16.3 %all_to_all.14 = s32[16,1,2]{2,1,0:T(1,128)S(1)} all-to-all(s32[16,1,2]{2,1,0:T(1,128)S(1)} %bitcast.52), channel_id=1, replica_groups=mesh['seq'=8,'batch'=16,'mp'=4] {'batch'}, dimensions={0} | all-to-all | bytes 256 | tf_op jit(solution)/shard_map/all_to_all | solution.py:54
  17.7 0.1 reshape.199
  17.8 0.0 copy-done
  17.8 4.4 %gather_fusion = bf16[32,128,896]{2,1,0:T(8,128)(2,1)} fusion(bf16[8,128,896]{2,1,0:T(8,128)(2,1)S(1)} %copy-done, s32[1024]{0:T(1024)S(1)} %pad_clamp_fusion.1), kind=kCustom, calls=%fused_computation | custom fusion | bytes 14680192 | tf_op jit(solution)/shard_map/gather | solution.py:52
  22.2 0.0 copy-start.3
  22.2 5.2 %all-to-all-start.1 = ((bf16[16,2,128,896]{3,2,1,0:T(8,128)(2,1)}), bf16[16,2,128,896]{3,2,1,0:T(8,128)(2,1)}, u32[]{:S(2)}, u32[]{:S(2)}) async-start(bf16[16,2,128,896]{3,2,1,0:T(8,128)(2,1)} %bitcast.46), calls=%async_computation.1 | async-start | bytes 14680064 | tf_op jit(solution)/shard_map/all_to_all | solution.py:57
  27.5 0.1 reshape_squeeze.12
  27.5 0.0 copy-done.3
  27.5 1.3 copy.39
  28.8 2.2 copy.40
  31.1 0.1 pad.10.clone
  31.2 157.3 %all-to-all-done.1 = bf16[16,2,128,896]{3,2,1,0:T(8,128)(2,1)} async-done(((bf16[16,2,128,896]{3,2,1,0:T(8,128)(2,1)}), bf16[16,2,128,896]{3,2,1,0:T(8,128)(2,1)}, u32[]{:S(2)}, u32[]{:S(2)}) %all-to-all-start.1) | async-done | bytes 7340064 | tf_op jit(solution)/shard_map/all_to_all | solution.py:57
  188.5 0.0 copy-start.4
  188.5 6.0 %gather_fusion.1 = bf16[16,128,896]{2,1,0:T(8,128)(2,1)} fusion(bf16[32,128,896]{2,1,0:T(8,128)(2,1)} %bitcast.6, s32[1024]{0:T(1024)S(1)} %pad_clamp_fusion), kind=kCustom, calls=%fused_computation.1 | custom fusion | bytes 7340096 | tf_op jit(solution)/shard_map/gather | solution.py:58
  194.6 0.0 copy-done.4
  194.6 6.5 %convert_bitcast_fusion = bf16[2,16,128,512]{2,3,1,0:T(8,128)(2,1)S(1)} fusion(bf16[16,128,896]{2,1,0:T(8,128)(2,1)} %gather_fusion.1, bf16[1,896,512]{1,2,0:T(8,128)(2,1)} %bitcast.50, bf16[1,896,512]{1,2,0:T(8,128)(2,1)S(1)} %bitcast.49), kind=kOutput, calls=%fused_computation.3 | convolution fusion | flops 3763863552 | bytes 9699328 | tf_op jit(solution)/shard_map/rne,kew->krnw/dot_general | solution.py:59
  201.1 0.0 copy-start.1
  201.1 1.9 copy-done.1
  203.0 0.0 copy-start.5
  203.0 0.1 copy.44
  203.2 0.1 slice.30
  203.3 0.1 copy.45
  203.5 0.1 slice.32
  203.6 0.8 pad_maximum_fusion
  204.4 3.9 %collective-permute-start = (bf16[2,256,4,128]{3,1,2,0:T(8,128)(2,1)}, bf16[2,256,4,128]{3,1,2,0:T(8,128)(2,1)}, u32[]{:S(2)}, u32[]{:S(2)}) collective-permute-start(bf16[2,256,4,128]{3,1,2,0:T(8,128)(2,1)} %pad_maximum_fusion), channel_id=1, source_target_pairs={{0,64},{64,128},{128,192},{192,256},{256,320},{320,384},{384,448},... | collective-permute-start | bytes 1572872 | tf_op jit(solution)/shard_map/ppermute | solution.py:12
  208.3 0.0 copy-done.5
  208.3 0.3 maximum_maximum_fusion
  208.6 0.1 reshape.195
  208.7 4.0 %fusion.41 = (bf16[1,16,128,512]{2,3,1,0:T(8,128)(2,1)S(1)}, bf16[1,16,128,512]{2,3,1,0:T(8,128)(2,1)}) fusion(bf16[2,16,128,512]{2,3,1,0:T(8,128)(2,1)} %copy-done.1), kind=kLoop, calls=%fused_computation.58 | loop fusion | bytes 8388608 | tf_op jit(solution)/shard_map/slice | solution.py:62
  212.7 2.7 %copy.50 = bf16[1,16,128,512]{2,1,3,0:T(8,128)(2,1)} copy(bf16[1,16,128,512]{2,3,1,0:T(8,128)(2,1)S(1)} %get-tuple-element.5) | data formatting | bytes 4194304 | tf_op jit(solution)/shard_map/slice | solution.py:62
  215.4 4.1 %reshape_squeeze.14 = bf16[8,256,4,128]{1,0,3,2:T(8,128)(2,1)} reshape(bf16[1,16,128,512]{2,1,3,0:T(8,128)(2,1)} %copy.50) | data formatting | bytes 4194304 | tf_op jit(solution)/shard_map/reshape;squeeze | solution.py:65
  219.5 4.5 %copy.51 = bf16[8,256,4,128]{3,1,2,0:T(8,128)(2,1)} copy(bf16[8,256,4,128]{1,0,3,2:T(8,128)(2,1)} %reshape_squeeze.14) | data formatting | bytes 4194304 | tf_op jit(solution)/shard_map/reshape;squeeze | solution.py:65
  224.0 4.2 %copy.48 = bf16[1,16,128,512]{2,1,3,0:T(8,128)(2,1)} copy(bf16[1,16,128,512]{2,3,1,0:T(8,128)(2,1)} %get-tuple-element.6) | data formatting | bytes 4194304 | tf_op jit(solution)/shard_map/slice | solution.py:63
  228.3 4.1 %reshape_squeeze.13 = bf16[8,256,4,128]{1,0,3,2:T(8,128)(2,1)} reshape(bf16[1,16,128,512]{2,1,3,0:T(8,128)(2,1)} %copy.48) | data formatting | bytes 4194304 | tf_op jit(solution)/shard_map/reshape;squeeze | solution.py:66
  232.3 4.5 %copy.49 = bf16[8,256,4,128]{3,1,2,0:T(8,128)(2,1)} copy(bf16[8,256,4,128]{1,0,3,2:T(8,128)(2,1)} %reshape_squeeze.13) | data formatting | bytes 4194304 | tf_op jit(solution)/shard_map/reshape;squeeze | solution.py:66
  236.9 0.0 collective-permute-done
  236.9 1.1 fusion.43
  238.0 2.5 %fusion.5 = f32[9,4,64,256]{3,2,1,0:T(8,128)S(1)} fusion(bf16[8,256,4,128]{3,1,2,0:T(8,128)(2,1)} %copy.51, bf16[1,256,4,128]{3,1,2,0:T(8,128)(2,1)S(1)} %get-tuple-element.9, bf16[9,64,4,128]{3,2,1,0:T(4,128)(2,1)S(1)} %reshape.195), kind=kOutput, calls=%fused_computation.6 | convolution fusion | flops 152174592 | bytes 5308416 | tf_op jit(solution)/shard_map/cqhd,ckhd->chqk/dot_general | solution.py:16
  240.5 0.0 copy-start.2
  240.5 1.4 copy-done.2
  241.9 1.0 fusion.44
  242.9 7.1 %fusion.21 = bf16[9,64,4,128]{3,1,2,0:T(8,128)(2,1)S(1)} fusion(bf16[8,256,4,128]{3,1,2,0:T(8,128)(2,1)} %copy.49, bf16[1,256,4,128]{3,1,2,0:T(8,128)(2,1)S(1)} %get-tuple-element.10, f32[9,4,64]{2,1,0:T(4,128)S(1)} %fusion.44, f32[9,4,64,256]{3,2,1,0:T(8,128)} %copy-done.2), kind=kOutput, calls=%fused_computation.22 | convolution fusion | flops 158960128 | bytes 5317632 | tf_op jit(solution)/shard_map/chqk,ckhd->cqhd/dot_general | solution.py:22
  250.0 0.5 copy.53
  250.5 0.1 copy.59
  250.6 0.9 slice_bitcast_fusion
  (11 shorter events, 0.2 us)
Async XLA Ops:
  0.0 17.8 %copy-start = (bf16[8,128,896]{2,1,0:T(8,128)(2,1)S(1)}, bf16[8,128,896]{2,1,0:T(8,128)(2,1)}, u32[]{:S(2)}) copy-start(bf16[8,128,896]{2,1,0:T(8,128)(2,1)} %param.7) | copy-start | bytes 5505028
  22.2 5.3 %copy-start.3 = (bf16[896,512]{1,0:T(8,128)(2,1)S(1)}, bf16[896,512]{1,0:T(8,128)(2,1)}, u32[]{:S(2)}) copy-start(bf16[896,512]{1,0:T(8,128)(2,1)} %param.8) | copy-start | bytes 2752516
  22.2 166.3 %all-to-all-start.1 = ((bf16[16,2,128,896]{3,2,1,0:T(8,128)(2,1)}), bf16[16,2,128,896]{3,2,1,0:T(8,128)(2,1)}, u32[]{:S(2)}, u32[]{:S(2)}) async-start(bf16[16,2,128,896]{3,2,1,0:T(8,128)(2,1)} %bitcast.46), calls=%async_computation.1 | async-start | bytes 14680064 | tf_op jit(solution)/shard_map/all_to_all | solution.py:57
  188.5 6.0 %copy-start.4 = (bf16[896,512]{0,1:T(8,128)(2,1)S(1)}, bf16[896,512]{0,1:T(8,128)(2,1)}, u32[]{:S(2)}) copy-start(bf16[896,512]{0,1:T(8,128)(2,1)} %copy.39) | copy-start | bytes 2752516
  201.1 1.9 copy-start.1
  203.0 5.3 %copy-start.5 = (bf16[1,512,512]{2,1,0:T(8,128)(2,1)S(1)}, bf16[1,512,512]{2,1,0:T(8,128)(2,1)}, u32[]{:S(2)}) copy-start(bf16[1,512,512]{2,1,0:T(8,128)(2,1)} %param.5) | copy-start | bytes 1572868
  204.4 32.5 %collective-permute-start = (bf16[2,256,4,128]{3,1,2,0:T(8,128)(2,1)}, bf16[2,256,4,128]{3,1,2,0:T(8,128)(2,1)}, u32[]{:S(2)}, u32[]{:S(2)}) collective-permute-start(bf16[2,256,4,128]{3,1,2,0:T(8,128)(2,1)} %pad_maximum_fusion), channel_id=1, source_target_pairs={{0,64},{64,128},{128,192},{192,256},{256,320},{320,384},{384,448},... | collective-permute-start | bytes 1572872 | tf_op jit(solution)/shard_map/ppermute | solution.py:12
  240.5 1.4 copy-start.2
where the time goes:
time: 252 us; the launch traced here: 251 us
  waiting for transfers between devices  157 us (62%)
  local copies, waits for them, and re-layouts  50 us (20%)
  blocking collectives  16.3 us (6%)
  matrix products  16.2 us (6%)
  starting transfers between devices  9.1 us (4%)
    all_to_all x1, waiting for transfers between devices, local(): lax.all_to_all(picked, 'batch', split_axis=0, concat_axis=0, tiled=True)  157 us
    all_to_all x1, blocking collectives, local(): lax.all_to_all(wanted_slots, 'batch', split_axis=0, concat_axis=0, tiled=...  16.3 us
    another operation x2, local copies, waits for them, and re-layouts, local(): group_keys = neigh_keys.reshape(num_groups, context_rows, heads_dev, DH)  8.62 us
    another operation x2, local copies, waits for them, and re-layouts, local(): group_values = neigh_values.reshape(num_groups, context_rows, heads_dev, DH)  8.6 us
    unnamed x16, local copies, waits for them, and re-layouts  7.85 us
    dot_general x1, matrix products, attend_groups(): jnp.einsum('chqk,ckhd->cqhd', weights, group_values, preferred_element_ty...  7.12 us
    slice x2, local copies, waits for them, and re-layouts, local(): neigh_keys = projected[0]  6.69 us
    dot_general x1, matrix products, local(): jnp.einsum('rne,kew->krnw', fetched, both_weights, preferred_element_type...  6.5 us
  transfers between devices with their start and end apart: 2, of which 1 were waited for; matrix products, arithmetic and copies ran while one was open for 13% of the time, Pallas kernels for 0%

commit v1 on v0

v1 whole, which is shorter than its diff:
```python
import functools

import jax
import jax.numpy as jnp
from jax import lax
from jax.experimental import pallas as pl
from jax.experimental.pallas import tpu as pltpu
from jax.sharding import PartitionSpec as P

MESH = pl.DeviceIdType.MESH
DH = 128
COL = 128
Y_CHUNKS = (0, 1, 2, 3, 4, 5, 6)
ORDER = (0, 1, 2, 3, 4, 5, 6)
LOOK = 1


def exchange_kernel(
    ids, q_hbm, e_hbm, wk_hbm, wv_hbm, o_ref,
    q_raw, e_own, wk, wv, table, asked, asked_s, packed, wide, q_pad, q_in, o_out, o_in,
    keys, values, acc, half0, half1, r0, r1, r2, r3, r4, r5, r6,
    load_sem, tab_send, tab_recv, tab_local, y_send, y_recv,
    to_right, to_left, from_left, from_right, on_right, on_left, opp_left, opp_right, edge_send, edge_recv,
):
    recv = (r0, r1, r2, r3, r4, r5, r6)
    halves = (half0, half1)
    z = lax.axis_index("seq")
    b = lax.axis_index("batch")
    x = lax.axis_index("mp")
    rows = e_own.shape[1]
    part = 8 * rows
    right = (z, b, lax.rem(x + 1, 4))
    left = (z, b, lax.rem(x + 3, 4))
    ahead = (lax.rem(z + 1, 8), b, x)
    behind = (lax.rem(z + 7, 8), b, x)

    def line(k):
        return lax.rem(b + k, 16)

    barrier = pltpu.get_barrier_semaphore()
    for device in (right, left, ahead, behind):
        pl.semaphore_signal(barrier, inc=1, device_id=device, device_id_type=MESH)

    def greet(k, carry):
        pl.semaphore_signal(barrier, inc=1, device_id=(z, line(k), x), device_id_type=MESH)
        return carry

    lax.fori_loop(1, 16, greet, 0)

    loads = [
        pltpu.make_async_copy(e_hbm.at[:, pl.ds(pl.multiple_of(x * rows, rows), rows), :], e_own, load_sem.at[0]),
        pltpu.make_async_copy(q_hbm.at[0], q_raw, load_sem.at[1]),
        pltpu.make_async_copy(wk_hbm, wk, load_sem.at[2]),
        pltpu.make_async_copy(wv_hbm, wv, load_sem.at[3]),
    ]
    for copy in loads:
        copy.start()

    lane = lax.broadcasted_iota(jnp.int32, (1, 128), 1)
    lane_owner = lax.shift_right_logical(lane, 1)
    lane_slot = lane & 1
    count = jnp.zeros((1, 128), jnp.int32)
    wanted = jnp.zeros((1, 128), jnp.int32)
    owners = []
    slot_of = []
    for s in range(16):
        one = ids[0, s // 2, s % 2]
        owner = lax.shift_right_logical(one, 3)
        same = lane_owner == owner
        wanted = jnp.where(same & (count == lane_slot), one & 7, wanted)
        count = count + same.astype(jnp.int32)
        rank = jnp.int32(0)
        for other in owners:
            rank = rank + (other == owner).astype(jnp.int32)
        owners.append(owner)
        slot_of.append(owner * 2 + jnp.minimum(rank, 1))
    table[...] = wanted

    loads[1].wait()
    wide[0:8, :] = jnp.zeros((8, wide.shape[1]), jnp.float32)
    wide[520:584, :] = jnp.zeros((64, wide.shape[1]), jnp.float32)
    for i in range(8):
        wide[8 + 64 * i : 72 + 64 * i, :] = q_raw[64 * i : 64 * i + 64, :].astype(jnp.float32)
    for i in range(9):
        q_pad[64 * i : 64 * i + 64, :] = wide[7 + 64 * i : 71 + 64 * i, :].astype(jnp.bfloat16)
    loads[0].wait()

    pl.semaphore_wait(barrier, 19)

    def tell(k, carry):
        pltpu.make_async_remote_copy(
            src_ref=table, dst_ref=asked.at[b], send_sem=tab_send, recv_sem=tab_recv,
            device_id=(z, line(k), x), device_id_type=MESH,
        ).start()
        return carry

    lax.fori_loop(1, 16, tell, 0)
    pltpu.make_async_copy(table, asked.at[b], tab_recv).start()
    edge_q = pltpu.make_async_remote_copy(
        src_ref=q_pad.at[pl.ds(0, 64)], dst_ref=q_in, send_sem=edge_send.at[0], recv_sem=edge_recv.at[0],
        device_id=behind, device_id_type=MESH,
    )
    edge_q.start()
    pltpu.make_async_copy(asked, asked, tab_recv).wait()
    to_scalar = pltpu.make_async_copy(asked, asked_s, tab_local)
    to_scalar.start()
    to_scalar.wait()

    for j in Y_CHUNKS:
        def serve(k, carry, j=j):
            to = line(k)
            for t in range(2):
                row = asked_s[to, 0, 2 * b + t]
                packed[j, k, t] = e_own[row, :, COL * j : COL * j + COL]
            pltpu.make_async_remote_copy(
                src_ref=packed.at[j, k], dst_ref=recv[j].at[pl.ds(2 * b, 2)],
                send_sem=y_send.at[j], recv_sem=y_recv.at[j],
                device_id=(z, to, x), device_id_type=MESH,
            ).start()
            return carry

        for t in range(2):
            row = asked_s[b, 0, 2 * b + t]
            packed[j, 0, t] = e_own[row, :, COL * j : COL * j + COL]
        pltpu.make_async_copy(packed.at[j, 0], recv[j].at[pl.ds(2 * b, 2)], y_recv.at[j]).start()
        lax.fori_loop(1, 16, serve, 0)

    units = [(h, j) for j in ORDER for h in (0, 1)]
    column = {j: pl.ds(COL * j, COL) for j in range(7)}

    def x_copy(h, j, src_row, dst_row, count, send, rcv, device):
        n = 7 * h + j
        return pltpu.make_async_remote_copy(
            src_ref=halves[h].at[pl.ds(src_row, count), column[j]],
            dst_ref=halves[h].at[pl.ds(dst_row, count), column[j]],
            send_sem=send.at[n], recv_sem=rcv.at[n], device_id=device, device_id_type=MESH,
        )

    def hop_right(h, j):
        return x_copy(h, j, 0, part, part, to_right, from_left, right)

    def hop_left(h, j):
        return x_copy(h, j, 0, 2 * part, part, to_left, from_right, left)

    def pass_right(h, j):
        return x_copy(h, j, part, 3 * part, part // 2, on_right, opp_left, right)

    def pass_left(h, j):
        return x_copy(h, j, 2 * part + part // 2, 3 * part + part // 2, part // 2, on_left, opp_right, left)

    def select_and_send(h, j):
        for s in range(8):
            slot = slot_of[8 * (1 - h) + s]
            halves[h][rows * s : rows * s + rows, COL * j : COL * j + COL] = recv[j][slot]
        hop_right(h, j).start()
        hop_left(h, j).start()

    def pass_on(h, j):
        hop_right(h, j).wait_recv()
        pass_right(h, j).start()
        hop_left(h, j).wait_recv()
        pass_left(h, j).start()

    def landed(h, j):
        pass_right(h, j).wait_recv()
        pass_left(h, j).wait_recv()

    group0 = (4, 0)

    def project_first(h):
        if h == 0:
            loads[2].wait()
            loads[3].wait()

        def body(i, carry):
            r = pl.ds(pl.multiple_of(i * part, part), part)
            lhs = halves[h][r, 0 : COL * 6]
            acc[h, r, 0:512] = jnp.dot(lhs, wk[0 : COL * 6, :], preferred_element_type=jnp.float32)
            acc[h, r, 512:1024] = jnp.dot(lhs, wv[0 : COL * 6, :], preferred_element_type=jnp.float32)
            return carry

        lax.fori_loop(0, 4, body, 0)

    def project_last(h):
        def body(i, carry):
            r = pl.ds(pl.multiple_of(i * part, part), part)
            to = pl.ds(pl.multiple_of(i * 2 * rows, 2 * rows), 2 * rows)
            lhs = halves[h][r, COL * 6 : COL * 7]
            k = acc[h, r, 0:512] + jnp.dot(lhs, wk[COL * 6 : COL * 7, :], preferred_element_type=jnp.float32)
            v = acc[h, r, 512:1024] + jnp.dot(lhs, wv[COL * 6 : COL * 7, :], preferred_element_type=jnp.float32)
            k = k.astype(jnp.bfloat16)
            v = v.astype(jnp.bfloat16)
            for g in range(4):
                keys[group0[h] + g, to, :] = k[2 * rows * g : 2 * rows * (g + 1), :]
                values[group0[h] + g, to, :] = v[2 * rows * g : 2 * rows * (g + 1), :]
            return carry

        lax.fori_loop(0, 4, body, 0)

    def attend(h):
        def body(i, carry):
            g = i + group0[h]
            r = pl.ds(pl.multiple_of(64 * g + 64, 64), 64)
            for n in range(4):
                c = slice(DH * n, DH * n + DH)
                scores = lax.dot_general(
                    q_pad[r, c], keys[g, :, c], (((1,), (1,)), ((), ())), preferred_element_type=jnp.float32
                ) * DH ** (-0.5)
                expon = jnp.exp(scores - jnp.max(scores, axis=-1, keepdims=True))
                weights = expon * (1.0 / jnp.sum(expon, axis=-1, keepdims=True))
                wide[r, c] = jnp.dot(
                    weights.astype(jnp.bfloat16), values[g, :, c], preferred_element_type=jnp.float32
                )
            return carry

        lax.fori_loop(0, 4, body, 0)

    edge_o = pltpu.make_async_remote_copy(
        src_ref=o_out, dst_ref=o_in, send_sem=edge_send.at[1], recv_sem=edge_recv.at[1],
        device_id=ahead, device_id_type=MESH,
    )

    def finish_half0():
        edge_q.wait_recv()
        row = lax.broadcasted_iota(jnp.int32, (64, 512), 0)
        q_pad[512:576, :] = jnp.where(
            row == 0, q_pad[512:576, :].astype(jnp.float32), q_in[...].astype(jnp.float32)
        ).astype(jnp.bfloat16)
        attend(0)
        o_out[...] = wide[512:576, :].astype(jnp.bfloat16)
        edge_o.start()

    done = {0: 0, 1: 0}

    def after(h, j):
        landed(h, j)
        done[h] += 1
        if done[h] == 6:
            project_first(h)
        if done[h] == 7:
            project_last(h)
            if h == 0:
                finish_half0()
            else:
                attend(1)

    seen = set()
    for n in range(len(units) + 2 * LOOK):
        if n < len(units):
            h, j = units[n]
            if j not in seen:
                seen.add(j)
                pltpu.make_async_copy(recv[j], recv[j], y_recv.at[j]).wait()
            select_and_send(h, j)
        if 0 <= n - LOOK < len(units):
            pass_on(*units[n - LOOK])
        if 0 <= n - 2 * LOOK < len(units):
            after(*units[n - 2 * LOOK])

    edge_o.wait_recv()
    wide[0:64, :] = jnp.where(z == 0, 0.0, o_in[...].astype(jnp.float32))
    for i in range(8):
        o_ref[0, 64 * i : 64 * i + 64, :] = wide[64 * i + 1 : 64 * i + 65, :].astype(jnp.bfloat16)

    edge_q.wait_send()
    edge_o.wait_send()
    pltpu.make_async_copy(asked.at[pl.ds(0, 15)], asked.at[pl.ds(0, 15)], tab_send).wait()
    for j in Y_CHUNKS:
        pltpu.make_async_copy(packed.at[j, pl.ds(0, 15)], packed.at[j, pl.ds(0, 15)], y_send.at[j]).wait()
    for h, j in units:
        hop_right(h, j).wait_send()
        hop_left(h, j).wait_send()
        pass_right(h, j).wait_send()
        pass_left(h, j).wait_send()


def local(queries, neighbour_ids, encoded, key_weight, value_weight):
    bf16, f32, i32 = jnp.bfloat16, jnp.float32, jnp.int32
    hbm = pl.BlockSpec(memory_space=pl.ANY)
    dma = pltpu.SemaphoreType.DMA
    return pl.pallas_call(
        exchange_kernel,
        out_shape=jax.ShapeDtypeStruct(queries.shape, bf16),
        in_specs=[pl.BlockSpec(memory_space=pltpu.SMEM), hbm, hbm, hbm, hbm],
        out_specs=pl.BlockSpec(memory_space=pltpu.VMEM),
        scratch_shapes=[
            pltpu.VMEM((512, 512), bf16),
            pltpu.VMEM((8, 32, 896), bf16),
            pltpu.VMEM((896, 512), bf16),
            pltpu.VMEM((896, 512), bf16),
            pltpu.VMEM((1, 128), i32),
            pltpu.VMEM((16, 1, 128), i32),
            pltpu.SMEM((16, 1, 128), i32),
            pltpu.VMEM((7, 16, 2, 32, 128), bf16),
            pltpu.VMEM((584, 512), f32),
            pltpu.VMEM((576, 512), bf16),
            pltpu.VMEM((64, 512), bf16),
            pltpu.VMEM((64, 512), bf16),
            pltpu.VMEM((64, 512), bf16),
            pltpu.VMEM((8, 256, 512), bf16),
            pltpu.VMEM((8, 256, 512), bf16),
            pltpu.VMEM((2, 1024, 1024), f32),
            pltpu.VMEM((1024, 896), bf16),
            pltpu.VMEM((1024, 896), bf16),
        ]
        + [pltpu.VMEM((32, 32, 128), bf16) for _ in range(7)]
        + [dma((4,)), dma, dma, dma, dma((7,)), dma((7,))]
        + [dma((14,)) for _ in range(8)]
        + [dma((2,)), dma((2,))],
        compiler_params=pltpu.CompilerParams(
            collective_id=0, has_side_effects=True, vmem_limit_bytes=48 * 2**20
        ),
        cost_estimate=pl.CostEstimate(flops=4_100_000_000, bytes_accessed=6_000_000, transcendentals=600_000),
    )(neighbour_ids, queries, encoded, key_weight, value_weight)


def solution(mesh):
    return jax.shard_map(
        local,
        mesh=mesh,
        in_specs=(
            P("batch", "seq", "mp"),
            P("batch", "seq", None),
            P("batch", None, None),
            P(None, "mp"),
            P(None, "mp"),
        ),
        out_specs=P("batch", "seq", "mp"),
        check_vma=False,
    )
```

time: 252 us -> 92.2 us (0.37)
  waiting for transfers between devices: 157 us -> 0 us
  Pallas kernels: 0 us -> 84 us
  local copies, waits for them, and re-layouts: 50 us -> 6.45 us
  blocking collectives: 16.3 us -> 0 us
  matrix products: 16.2 us -> 0 us
  starting transfers between devices: 9.1 us -> 0 us
    all_to_all x1 -> x0, waiting for transfers between devices: 157 us -> none  [local(): lax.all_to_all(picked, 'batch', split_axis=0, concat_axis=0, tiled=True)]
    pallas_call x0 -> x1, Pallas kernels: none -> 84 us  [local(): pl.pallas_call(exchange_kernel, out_shape=jax.ShapeDtypeStruct(queries.sh...]
    another operation x6 -> x0, local copies, waits for them, and re-layouts: 17.4 us -> none  [the longest x2 8.62 us: local(): group_keys = neigh_keys.reshape(num_groups, context_rows, heads_dev, DH)]
    all_to_all x1 -> x0, blocking collectives: 16.3 us -> none  [local(): lax.all_to_all(wanted_slots, 'batch', split_axis=0, concat_axis=0, tiled=...]
    dot_general x3 -> x0, matrix products: 16.2 us -> none  [the longest x1 7.12 us: attend_groups(): jnp.einsum('chqk,ckhd->cqhd', weights, group_values, preferred_element_ty...]
    slice x11 -> x0, local copies, waits for them, and re-layouts: 12.5 us -> none  [the longest x2 6.69 us: local(): neigh_keys = projected[0]]
    gather x2 -> x0, local copies, waits for them, and re-layouts: 10.4 us -> none  [the longest x1 6.03 us: local(): fetched = fetched.reshape(owners * capacity, nlen_rows, enc_width)[slot_of]]
    all_to_all x1 -> x0, starting transfers between devices: 5.22 us -> none  [local(): lax.all_to_all(picked, 'batch', split_axis=0, concat_axis=0, tiled=True)]
  transfers between devices with their start and end apart: 2 -> 0, of which waited for: 1 -> 0; matrix products, arithmetic and copies ran while one was open for 13% -> 0% of each run, Pallas kernels for 0% -> 0%
where the time goes in v1:
time: 92.2 us; the launch traced here: 90.4 us
  Pallas kernels  84 us (91%)
  local copies, waits for them, and re-layouts  6.45 us (7%)
    pallas_call x1, Pallas kernels, local(): pl.pallas_call(exchange_kernel, out_shape=jax.ShapeDtypeStruct(queries.sh...  84 us
    unnamed x10, local copies, waits for them, and re-layouts  6.45 us

profile of v1, /device:TPU:1, one launch (start us, length us, event | category | flops | bytes accessed | tf_op | source)
XLA Modules:
  0.0 90.4 jit_solution(17305298012874153996)
XLA Ops:
  0.0 0.8 copy.6.ids
  0.8 0.0 copy-start
  0.8 1.5 %copy-done = bf16[8,128,896]{2,1,0:T(8,128)(2,1)S(1)} copy-done((bf16[8,128,896]{2,1,0:T(8,128)(2,1)S(1)}, bf16[8,128,896]{2,1,0:T(8,128)(2,1)}, u32[]{:S(2)}) %copy-start) | copy-done | bytes 1835032
  2.3 0.0 copy-start.1
  2.3 1.2 %copy-done.1 = bf16[896,512]{1,0:T(8,128)(2,1)S(1)} copy-done((bf16[896,512]{1,0:T(8,128)(2,1)S(1)}, bf16[896,512]{1,0:T(8,128)(2,1)}, u32[]{:S(2)}) %copy-start.1) | copy-done | bytes 917528
  3.4 0.0 copy-start.2
  3.4 1.2 %copy-done.2 = bf16[896,512]{1,0:T(8,128)(2,1)S(1)} copy-done((bf16[896,512]{1,0:T(8,128)(2,1)S(1)}, bf16[896,512]{1,0:T(8,128)(2,1)}, u32[]{:S(2)}) %copy-start.2) | copy-done | bytes 917528
  4.6 0.0 copy-start.3
  4.6 1.0 %copy-done.3 = bf16[1,512,512]{2,1,0:T(8,128)(2,1)S(1)} copy-done((bf16[1,512,512]{2,1,0:T(8,128)(2,1)S(1)}, bf16[1,512,512]{2,1,0:T(8,128)(2,1)}, u32[]{:S(2)}) %copy-start.3) | copy-done | bytes 524312
  5.7 84.0 %shard_map.55 = bf16[1,512,512]{2,1,0:T(8,128)(2,1)S(1)} custom-call(s32[1,8,2]{2,1,0:T(8,128)S(1)} %copy.6.ids, bf16[1,512,512]{2,1,0:T(8,128)(2,1)S(1)} %copy-done.3, bf16[8,128,896]{2,1,0:T(8,128)(2,1)S(1)} %copy-done, bf16[896,512]{1,0:T(8,128)(2,1)S(1)} %copy-done.1, bf16[896,512]{1,0:T(8,128)(2,1)S(1)} %copy-done.2), custom_call_target="tpu_custom_call" | custom-call | flops 4100000000 | bytes 6000000 | tf_op jit(solution)/shard_map/pallas_call | solution.py:281
  89.6 0.8 copy.8
Async XLA Ops:
  0.8 1.5 %copy-start = (bf16[8,128,896]{2,1,0:T(8,128)(2,1)S(1)}, bf16[8,128,896]{2,1,0:T(8,128)(2,1)}, u32[]{:S(2)}) copy-start(bf16[8,128,896]{2,1,0:T(8,128)(2,1)} %e_hbm.1) | copy-start | bytes 5505028
  2.3 1.2 %copy-start.1 = (bf16[896,512]{1,0:T(8,128)(2,1)S(1)}, bf16[896,512]{1,0:T(8,128)(2,1)}, u32[]{:S(2)}) copy-start(bf16[896,512]{1,0:T(8,128)(2,1)} %wk_hbm.1) | copy-start | bytes 2752516
  3.4 1.2 %copy-start.2 = (bf16[896,512]{1,0:T(8,128)(2,1)S(1)}, bf16[896,512]{1,0:T(8,128)(2,1)}, u32[]{:S(2)}) copy-start(bf16[896,512]{1,0:T(8,128)(2,1)} %wv_hbm.1) | copy-start | bytes 2752516
  4.6 1.0 %copy-start.3 = (bf16[1,512,512]{2,1,0:T(8,128)(2,1)S(1)}, bf16[1,512,512]{2,1,0:T(8,128)(2,1)}, u32[]{:S(2)}) copy-start(bf16[1,512,512]{2,1,0:T(8,128)(2,1)} %q_hbm.1) | copy-start | bytes 1572868

commit v2 on v1

v2 whole, which is shorter than its diff:
```python
import jax
import jax.numpy as jnp
from jax import lax
from jax.experimental import pallas as pl
from jax.experimental.pallas import tpu as pltpu
from jax.sharding import PartitionSpec as P

MESH = pl.DeviceIdType.MESH
DH = 128
EXP2_SCALE = DH ** (-0.5) * 1.4426950408889634
COL = 128
Z_CHUNKS = (3, 4, 5)
Z_FIRST = 3
SERVE = (0, 1, 3, 2, 4, 5, 6)
UPFRONT = 3
PARTS = ((4, 5, 6, 7), (0, 1, 2, 3))
UNITS = (
    (0, 0), (1, 0), (0, 1), (0, 3), (1, 1), (0, 2), (1, 3), (0, 4), (0, 5), (0, 6), (1, 2), (1, 4), (1, 5), (1, 6),
)
LOOK = 3


def exchange_kernel(
    ids, q_hbm, e_hbm, wk_hbm, wv_hbm, o_ref,
    q_raw, e_own, e_line, wk, wv, table, asked_y, asked_z, asked_y_s, asked_z_s, packed, wide, q_pad, q_in, o_out, o_in,
    keys, values, scores, weights, acc0, acc1, part0, part1, r0, r1, r2, r3, r4, r5, r6,
    load_sem, tab_send, tab_recv, tab_local, pre_send, pre_recv, serve_send, serve_recv,
    to_right, to_left, from_left, from_right, on_right, on_left, opp_left, opp_right, edge_send, edge_recv,
):
    recv = (r0, r1, r2, r3, r4, r5, r6)
    parts = (part0, part1)
    accs = (acc0, acc1)
    z = lax.axis_index("seq")
    b = lax.axis_index("batch")
    x = lax.axis_index("mp")
    y = lax.div(b, 2)
    core = lax.rem(b, 2)
    zc = 2 * z + core
    rows = e_own.shape[1]
    right = (z, b, lax.rem(x + 1, 4))
    left = (z, b, lax.rem(x + 3, 4))
    ahead = (lax.rem(z + 1, 8), b, x)
    behind = (lax.rem(z + 7, 8), b, x)

    def y_line(k):
        to = lax.rem(b + k, 16)
        return to, (z, to, x)

    def z_line(k):
        to = lax.rem(zc + k, 16)
        return to, (lax.div(to, 2), 2 * y + lax.rem(to, 2), x)

    barrier = pltpu.get_barrier_semaphore()

    def greet_one(device):
        pl.semaphore_signal(barrier, inc=1, device_id=device, device_id_type=MESH)

    greet_one(right)
    greet_one(left)

    def greet(k, carry):
        greet_one(y_line(k)[1])
        greet_one(z_line(k)[1])
        return carry

    lax.fori_loop(1, 16, greet, 0)

    def greet_source(k, carry):
        greet_one((lax.rem(z + k, 8), zc, x))
        return carry

    lax.fori_loop(1, 8, greet_source, 0)

    @pl.when(y != z)
    def _():
        greet_one((z, zc, x))

    loads = [
        pltpu.make_async_copy(e_hbm.at[:, pl.ds(pl.multiple_of(x * rows, rows), rows), :], e_own, load_sem.at[0]),
        pltpu.make_async_copy(q_hbm.at[0], q_raw, load_sem.at[1]),
        pltpu.make_async_copy(wk_hbm, wk, load_sem.at[2]),
        pltpu.make_async_copy(wv_hbm, wv, load_sem.at[3]),
    ]
    for copy in loads:
        copy.start()

    lane = lax.broadcasted_iota(jnp.int32, (1, 128), 1)
    lane_owner = lax.shift_right_logical(lane, 1)
    lane_slot = lane & 1
    count = jnp.zeros((1, 128), jnp.int32)
    wanted = jnp.zeros((1, 128), jnp.int32)
    owners = []
    slot_of = []
    for s in range(16):
        one = ids[0, s % 2, s // 2]
        owner = lax.shift_right_logical(one, 3)
        same = lane_owner == owner
        wanted = jnp.where(same & (count == lane_slot), one & 7, wanted)
        count = count + same.astype(jnp.int32)
        rank = jnp.int32(0)
        for other in owners:
            rank = rank + (other == owner).astype(jnp.int32)
        owners.append(owner)
        slot_of.append(owner * 2 + jnp.minimum(rank, 1))
    table[...] = wanted
    loads[0].wait()

    pl.semaphore_wait(barrier, 39 + (y != z).astype(jnp.int32))

    def tell(line, asked, n, me):
        def body(k, carry):
            pltpu.make_async_remote_copy(
                src_ref=table, dst_ref=asked.at[me], send_sem=tab_send.at[n], recv_sem=tab_recv.at[n],
                device_id=line(k)[1], device_id_type=MESH,
            ).start()
            return carry

        lax.fori_loop(1, 16, body, 0)
        pltpu.make_async_copy(table, asked.at[me], tab_recv.at[n]).start()

    tell(y_line, asked_y, 0, b)
    tell(z_line, asked_z, 1, zc)

    z_cols = pl.ds(COL * Z_FIRST, COL * len(Z_CHUNKS))

    def spread(k, send):
        return pltpu.make_async_remote_copy(
            src_ref=e_own.at[z, :, z_cols], dst_ref=e_line.at[z], send_sem=pre_send.at[send], recv_sem=pre_recv,
            device_id=(y, 2 * lax.rem(y + k, 8) + core, x), device_id_type=MESH,
        )

    def spread_one(k, carry):
        spread(k, 0).start()
        return carry

    lax.fori_loop(1, 8, spread_one, 0)

    @pl.when(y != z)
    def _():
        spread(0, 1).start()

    @pl.when(y == z)
    def _():
        pltpu.make_async_copy(e_own.at[z, :, z_cols], e_line.at[z], pre_recv).start()

    loads[1].wait()
    wide[0:8, :] = jnp.zeros((8, wide.shape[1]), jnp.float32)
    wide[520:584, :] = jnp.zeros((64, wide.shape[1]), jnp.float32)
    for i in range(8):
        wide[8 + 64 * i : 72 + 64 * i, :] = q_raw[64 * i : 64 * i + 64, :].astype(jnp.float32)
    for i in range(9):
        q_pad[64 * i : 64 * i + 64, :] = wide[7 + 64 * i : 71 + 64 * i, :].astype(jnp.bfloat16)
    edge_q = pltpu.make_async_remote_copy(
        src_ref=q_pad.at[pl.ds(0, 64)], dst_ref=q_in, send_sem=edge_send.at[0], recv_sem=edge_recv.at[0],
        device_id=behind, device_id_type=MESH,
    )
    edge_q.start()
    for g in range(8):
        for m in range(4):
            values[g, :, 2 * DH * m + DH : 2 * DH * m + 2 * DH] = jnp.ones((256, DH), jnp.bfloat16)
    scalars = []
    for n, (asked, asked_s) in enumerate(((asked_y, asked_y_s), (asked_z, asked_z_s))):
        pltpu.make_async_copy(asked, asked, tab_recv.at[n]).wait()
        scalars.append(pltpu.make_async_copy(asked, asked_s, tab_local.at[n]))
        scalars[n].start()
    scalars[0].wait()

    def serve(j):
        if j in Z_CHUNKS:
            block, col, asked_s, me, line = e_line, COL * (j - Z_FIRST), asked_z_s, zc, z_line
            if j == Z_CHUNKS[0]:
                scalars[1].wait()
                pltpu.make_async_copy(e_line, e_line, pre_recv).wait()
        else:
            block, col, asked_s, me, line = e_own, COL * j, asked_y_s, b, y_line

        def pack(k, to):
            for t in range(2):
                packed[j, k, t] = block[asked_s[to, 0, 2 * me + t], :, col : col + COL]

        def body(k, carry):
            to, device = line(k)
            pack(k, to)
            pltpu.make_async_remote_copy(
                src_ref=packed.at[j, k], dst_ref=recv[j].at[pl.ds(2 * me, 2)],
                send_sem=serve_send.at[j], recv_sem=serve_recv.at[j], device_id=device, device_id_type=MESH,
            ).start()
            return carry

        lax.fori_loop(1, 16, body, 0)
        pack(0, me)
        pltpu.make_async_copy(packed.at[j, 0], recv[j].at[pl.ds(2 * me, 2)], serve_recv.at[j]).start()

    def x_copy(p, j, src_row, dst_row, count, send, rcv, device):
        return pltpu.make_async_remote_copy(
            src_ref=parts[p].at[j, pl.ds(src_row, count)],
            dst_ref=parts[p].at[j, pl.ds(dst_row, count)],
            send_sem=send.at[p, j], recv_sem=rcv.at[p, j], device_id=device, device_id_type=MESH,
        )

    def quarter(p):
        return 2 * rows * len(PARTS[p])

    def hop_right(p, j):
        return x_copy(p, j, 0, quarter(p), quarter(p), to_right, from_left, right)

    def hop_left(p, j):
        return x_copy(p, j, 0, 2 * quarter(p), quarter(p), to_left, from_right, left)

    def pass_right(p, j):
        return x_copy(p, j, quarter(p), 3 * quarter(p), quarter(p) // 2, on_right, opp_left, right)

    def pass_left(p, j):
        n = quarter(p) // 2
        return x_copy(p, j, 5 * n, 7 * n, n, on_left, opp_right, left)

    def select_and_send(p, j):
        n = 0
        for g in PARTS[p]:
            for s in (2 * g, 2 * g + 1):
                parts[p][j, rows * n : rows * n + rows, :] = recv[j][slot_of[s]]
                n += 1
        hop_right(p, j).start()
        hop_left(p, j).start()

    def pass_on(p, j):
        hop_right(p, j).wait_recv()
        pass_right(p, j).start()
        hop_left(p, j).wait_recv()
        pass_left(p, j).start()

    def project_first(p):
        def body(i, carry):
            r = pl.ds(pl.multiple_of(i * quarter(p), quarter(p)), quarter(p))
            lhs = jnp.concatenate([parts[p][j, r, :] for j in range(6)], axis=1)
            accs[p][r, 0:512] = jnp.dot(lhs, wk[0 : COL * 6, :], preferred_element_type=jnp.float32)
            accs[p][r, 512:1024] = jnp.dot(lhs, wv[0 : COL * 6, :], preferred_element_type=jnp.float32)
            return carry

        lax.fori_loop(0, 4, body, 0)

    def project_last(p):
        def body(i, carry):
            r = pl.ds(pl.multiple_of(i * quarter(p), quarter(p)), quarter(p))
            to = pl.ds(pl.multiple_of(i * 2 * rows, 2 * rows), 2 * rows)
            lhs = parts[p][6, r, :]
            k = accs[p][r, 0:512] + jnp.dot(lhs, wk[COL * 6 : COL * 7, :], preferred_element_type=jnp.float32)
            v = accs[p][r, 512:1024] + jnp.dot(lhs, wv[COL * 6 : COL * 7, :], preferred_element_type=jnp.float32)
            k = k.astype(jnp.bfloat16)
            v = v.astype(jnp.bfloat16)
            for n, g in enumerate(PARTS[p]):
                keys[g, to, :] = k[2 * rows * n : 2 * rows * (n + 1), :]
                for m in range(4):
                    values[g, to, 2 * DH * m : 2 * DH * m + DH] = v[
                        2 * rows * n : 2 * rows * (n + 1), DH * m : DH * m + DH
                    ]
            return carry

        lax.fori_loop(0, 4, body, 0)

    def attend(p):
        first = PARTS[p][0]
        heads = [slice(DH * n, DH * n + DH) for n in range(4)]
        wider = [slice(2 * DH * n, 2 * DH * n + 2 * DH) for n in range(4)]

        def block(i):
            return pl.ds(pl.multiple_of(64 * (i + first) + 64, 64), 64)

        def score(i, carry):
            for n in range(4):
                scores[i, n] = lax.dot_general(
                    q_pad[block(i), heads[n]], keys[i + first, :, heads[n]], (((1,), (1,)), ((), ())),
                    preferred_element_type=jnp.float32,
                )
            return carry

        def weigh(i, carry):
            for n in range(4):
                one = scores[i, n]
                top = jnp.max(one, axis=-1, keepdims=True)
                weights[i, n] = jnp.exp2((one - top) * EXP2_SCALE).astype(jnp.bfloat16)
            return carry

        def mix(i, carry):
            for n in range(4):
                both = jnp.dot(weights[i, n], values[i + first, :, wider[n]], preferred_element_type=jnp.float32)
                wide[block(i), heads[n]] = both[:, :DH] / both[:, DH:]
            return carry

        for step in (score, weigh, mix):
            lax.fori_loop(0, len(PARTS[p]), step, 0, unroll=True)

    edge_o = pltpu.make_async_remote_copy(
        src_ref=o_out, dst_ref=o_in, send_sem=edge_send.at[1], recv_sem=edge_recv.at[1],
        device_id=ahead, device_id_type=MESH,
    )

    def write_out(blocks):
        for i in blocks:
            o_ref[0, 64 * i : 64 * i + 64, :] = wide[64 * i + 1 : 64 * i + 65, :].astype(jnp.bfloat16)

    done = [0] * len(PARTS)

    def landed(p, j):
        pass_right(p, j).wait_recv()
        pass_left(p, j).wait_recv()
        done[p] += 1
        if done[p] == 6:
            if p == 0:
                loads[2].wait()
                loads[3].wait()
            project_first(p)
        if done[p] == 7:
            project_last(p)
            if p == 0:
                edge_q.wait_recv()
                row = lax.broadcasted_iota(jnp.int32, (64, 512), 0)
                q_pad[512:576, :] = jnp.where(
                    row == 0, q_pad[512:576, :].astype(jnp.float32), q_in[...].astype(jnp.float32)
                ).astype(jnp.bfloat16)
            attend(p)
            if p == 0:
                o_out[...] = wide[512:576, :].astype(jnp.bfloat16)
                edge_o.start()
                write_out((5, 6, 7))

    for j in SERVE[:UPFRONT]:
        serve(j)
    served = UPFRONT
    seen = set()
    for n in range(len(UNITS) + 2 * LOOK):
        if n < len(UNITS):
            p, j = UNITS[n]
            if j not in seen:
                seen.add(j)
                pltpu.make_async_copy(recv[j], recv[j], serve_recv.at[j]).wait()
            select_and_send(p, j)
            if served < len(SERVE):
                serve(SERVE[served])
                served += 1
        if 0 <= n - LOOK < len(UNITS):
            pass_on(*UNITS[n - LOOK])
        if 0 <= n - 2 * LOOK < len(UNITS):
            if n - 2 * LOOK == len(UNITS) - 1:
                edge_q.wait_send()
                edge_o.wait_send()
                for i, asked in enumerate((asked_y, asked_z)):
                    pltpu.make_async_copy(asked.at[pl.ds(0, 15)], asked.at[pl.ds(0, 15)], tab_send.at[i]).wait()
                pltpu.make_async_copy(e_line.at[pl.ds(0, 7)], e_line.at[pl.ds(0, 7)], pre_send.at[0]).wait()

                @pl.when(y != z)
                def _():
                    spread(0, 1).wait_send()

                for j in SERVE:
                    sent = packed.at[j, pl.ds(1, 15)]
                    pltpu.make_async_copy(sent, sent, serve_send.at[j]).wait()
                for p, j in UNITS:
                    hop_right(p, j).wait_send()
                    hop_left(p, j).wait_send()
                    pass_right(p, j).wait_send()
                    pass_left(p, j).wait_send()
                edge_o.wait_recv()
                wide[0:64, :] = jnp.where(z == 0, 0.0, o_in[...].astype(jnp.float32))
            landed(*UNITS[n - 2 * LOOK])
    write_out((0, 1, 2, 3, 4))


def local(queries, neighbour_ids, encoded, key_weight, value_weight):
    bf16, f32, i32 = jnp.bfloat16, jnp.float32, jnp.int32
    hbm = pl.BlockSpec(memory_space=pl.ANY)
    dma = pltpu.SemaphoreType.DMA
    part_rows = [256 * len(groups) for groups in PARTS]
    return pl.pallas_call(
        exchange_kernel,
        out_shape=jax.ShapeDtypeStruct(queries.shape, bf16),
        in_specs=[pl.BlockSpec(memory_space=pltpu.SMEM), hbm, hbm, hbm, hbm],
        out_specs=pl.BlockSpec(memory_space=pltpu.VMEM),
        scratch_shapes=[
            pltpu.VMEM((512, 512), bf16),
            pltpu.VMEM((8, 32, 896), bf16),
            pltpu.VMEM((8, 32, COL * len(Z_CHUNKS)), bf16),
            pltpu.VMEM((896, 512), bf16),
            pltpu.VMEM((896, 512), bf16),
            pltpu.VMEM((1, 128), i32),
            pltpu.VMEM((16, 1, 128), i32),
            pltpu.VMEM((16, 1, 128), i32),
            pltpu.SMEM((16, 1, 128), i32),
            pltpu.SMEM((16, 1, 128), i32),
            pltpu.VMEM((7, 16, 2, 32, 128), bf16),
            pltpu.VMEM((584, 512), f32),
            pltpu.VMEM((576, 512), bf16),
            pltpu.VMEM((64, 512), bf16),
            pltpu.VMEM((64, 512), bf16),
            pltpu.VMEM((64, 512), bf16),
            pltpu.VMEM((8, 256, 512), bf16),
            pltpu.VMEM((8, 256, 1024), bf16),
            pltpu.VMEM((4, 4, 64, 256), f32),
            pltpu.VMEM((4, 4, 64, 256), bf16),
        ]
        + [pltpu.VMEM((n, 1024), f32) for n in part_rows]
        + [pltpu.VMEM((7, n, COL), bf16) for n in part_rows]
        + [pltpu.VMEM((32, 32, 128), bf16) for _ in range(7)]
        + [dma((4,)), dma((2,)), dma((2,)), dma((2,)), dma((2,)), dma, dma((7,)), dma((7,))]
        + [dma((len(PARTS), 7)) for _ in range(8)]
        + [dma((2,)), dma((2,))],
        compiler_params=pltpu.CompilerParams(
            collective_id=0, has_side_effects=True, vmem_limit_bytes=60 * 2**20
        ),
        cost_estimate=pl.CostEstimate(flops=4_100_000_000, bytes_accessed=6_000_000, transcendentals=600_000),
    )(jnp.transpose(neighbour_ids, (0, 2, 1)), queries, encoded, key_weight, value_weight)


def solution(mesh):
    return jax.shard_map(
        local,
        mesh=mesh,
        in_specs=(
            P("batch", "seq", "mp"),
            P("batch", "seq", None),
            P("batch", None, None),
            P(None, "mp"),
            P(None, "mp"),
        ),
        out_specs=P("batch", "seq", "mp"),
        check_vma=False,
    )
```

time: 92.2 us -> 74.8 us (0.81)
  Pallas kernels: 84 us -> 71.6 us
  local copies, waits for them, and re-layouts: 6.45 us -> 1.87 us
    pallas_call x1, Pallas kernels: 84 us -> 71.6 us  [local(): pl.pallas_call(exchange_kernel, out_shape=jax.ShapeDtypeStruct(queries.sh...]
    unnamed x10 -> x1, local copies, waits for them, and re-layouts: 6.45 us -> 1.87 us
where the time goes in v2:
time: 74.8 us; the launch traced here: 73.4 us
  Pallas kernels  71.6 us (96%)
  local copies, waits for them, and re-layouts  1.87 us (2%)
    pallas_call x1, Pallas kernels, local(): pl.pallas_call(exchange_kernel, out_shape=jax.ShapeDtypeStruct(queries.sh...  71.6 us
    unnamed x1, local copies, waits for them, and re-layouts  1.87 us

profile of v2, /device:TPU:1, one launch (start us, length us, event | category | flops | bytes accessed | tf_op | source)
XLA Modules:
  0.0 73.4 jit_solution(6621685301881005043)
XLA Ops:
  0.0 71.6 %shard_map.55 = bf16[1,512,512]{2,1,0:T(8,128)(2,1)} custom-call(s32[1,2,8]{2,1,0:T(2,128)} %bitcast.1, bf16[1,512,512]{2,1,0:T(8,128)(2,1)} %q_hbm.1, bf16[8,128,896]{2,1,0:T(8,128)(2,1)} %e_hbm.1, bf16[896,512]{1,0:T(8,128)(2,1)} %wk_hbm.1, bf16[896,512]{1,0:T(8,128)(2,1)} %wv_hbm.1), custom_call_target="tpu_custom_call" | custom-call | flops 4100000000 | bytes 6000000 | tf_op jit(solution)/shard_map/pallas_call | solution.py:374
  71.6 1.9 %copy.7 = bf16[1,512,512]{2,1,0:T(8,128)(2,1)} copy(bf16[1,512,512]{2,1,0:T(8,128)(2,1)} %shard_map.55) | data formatting | bytes 1048576

commit v3 on v2

--- a/solution.py
+++ b/solution.py
@@ -9,25 +9,42 @@
 DH = 128
 EXP2_SCALE = DH ** (-0.5) * 1.4426950408889634
 COL = 128
-Z_CHUNKS = (3, 4, 5)
+PIECES = ((0, 0), (0, 1), (1, None), (2, None), (6, None), (3, None), (4, None), (5, None))
+Y_PIECES = 5
 Z_FIRST = 3
-SERVE = (0, 1, 3, 2, 4, 5, 6)
-UPFRONT = 3
+Z_COUNT = 3
+SERVE = (0, 1, 2, 5, 3, 6, 7, 4)
 PARTS = ((4, 5, 6, 7), (0, 1, 2, 3))
-UNITS = (
-    (0, 0), (1, 0), (0, 1), (0, 3), (1, 1), (0, 2), (1, 3), (0, 4), (0, 5), (0, 6), (1, 2), (1, 4), (1, 5), (1, 6),
-)
-LOOK = 3
+UNITS = ((0, 0), (1, 0), (0, 1), (1, 1), (0, 5), (0, 2), (1, 5), (0, 6), (0, 3), (0, 7), (1, 2), (0, 4), (1, 6), (1, 3), (1, 7), (1, 4))
+PASS_LAG = 4
+SEE_LAG = 8
+
+
+def make_plan():
+    plan = [("serve", i) for i in SERVE]
+    for n in range(len(UNITS) + SEE_LAG):
+        if 0 <= n - PASS_LAG < len(UNITS):
+            plan.append(("pass",) + UNITS[n - PASS_LAG])
+        if n < len(UNITS):
+            plan.append(("take",) + UNITS[n])
+        if n >= SEE_LAG:
+            plan.append(("see",) + UNITS[n - SEE_LAG])
+    return plan
+
+
+PLAN = make_plan()
 
 
 def exchange_kernel(
     ids, q_hbm, e_hbm, wk_hbm, wv_hbm, o_ref,
-    q_raw, e_own, e_line, wk, wv, table, asked_y, asked_z, asked_y_s, asked_z_s, packed, wide, q_pad, q_in, o_out, o_in,
-    keys, values, scores, weights, acc0, acc1, part0, part1, r0, r1, r2, r3, r4, r5, r6,
+    q_raw, e_own, e_line, wk, wv, table, asked_y, asked_z, asked_y_s, asked_z_s, wide, q_pad, q_in, o_out, o_in,
+    keys, values, scores, weights, acc0, acc1, part0, part1, r0, r1, r2, r3, r4, r5, r6, r7,
+    d0, d1, d2, d3, d4, d5, d6, d7,
     load_sem, tab_send, tab_recv, tab_local, pre_send, pre_recv, serve_send, serve_recv,
     to_right, to_left, from_left, from_right, on_right, on_left, opp_left, opp_right, edge_send, edge_recv,
 ):
-    recv = (r0, r1, r2, r3, r4, r5, r6)
+    recv = (r0, r1, r2, r3, r4, r5, r6, r7)
+    packed = (d0, d1, d2, d3, d4, d5, d6, d7)
     parts = (part0, part1)
     accs = (acc0, acc1)
     z = lax.axis_index("seq")
@@ -121,7 +138,7 @@
     tell(y_line, asked_y, 0, b)
     tell(z_line, asked_z, 1, zc)
 
-    z_cols = pl.ds(COL * Z_FIRST, COL * len(Z_CHUNKS))
+    z_cols = pl.ds(COL * Z_FIRST, COL * Z_COUNT)
 
     def spread(k, send):
         return pltpu.make_async_remote_copy(
@@ -160,74 +177,91 @@
             values[g, :, 2 * DH * m + DH : 2 * DH * m + 2 * DH] = jnp.ones((256, DH), jnp.bfloat16)
     scalars = []
     for n, (asked, asked_s) in enumerate(((asked_y, asked_y_s), (asked_z, asked_z_s))):
+        scalars.append(pltpu.make_async_copy(asked, asked_s, tab_local.at[n]))
+
+    def know(n, asked):
         pltpu.make_async_copy(asked, asked, tab_recv.at[n]).wait()
-        scalars.append(pltpu.make_async_copy(asked, asked_s, tab_local.at[n]))
         scalars[n].start()
-    scalars[0].wait()
-
-    def serve(j):
-        if j in Z_CHUNKS:
+        scalars[n].wait()
+
+    know(0, asked_y)
+
+    def serve(i):
+        j, half = PIECES[i]
+        if i >= Y_PIECES:
             block, col, asked_s, me, line = e_line, COL * (j - Z_FIRST), asked_z_s, zc, z_line
-            if j == Z_CHUNKS[0]:
-                scalars[1].wait()
+            if i == Y_PIECES:
+                know(1, asked_z)
                 pltpu.make_async_copy(e_line, e_line, pre_recv).wait()
         else:
             block, col, asked_s, me, line = e_own, COL * j, asked_y_s, b, y_line
+        first, count = (0, rows) if half is None else (half * rows // 2, rows // 2)
 
         def pack(k, to):
             for t in range(2):
-                packed[j, k, t] = block[asked_s[to, 0, 2 * me + t], :, col : col + COL]
+                packed[i][k, t] = block[asked_s[to, 0, 2 * me + t], first : first + count, col : col + COL]
 
         def body(k, carry):
             to, device = line(k)
             pack(k, to)
             pltpu.make_async_remote_copy(
-                src_ref=packed.at[j, k], dst_ref=recv[j].at[pl.ds(2 * me, 2)],
-                send_sem=serve_send.at[j], recv_sem=serve_recv.at[j], device_id=device, device_id_type=MESH,
+                src_ref=packed[i].at[k], dst_ref=recv[i].at[pl.ds(2 * me, 2)],
+                send_sem=serve_send.at[i], recv_sem=serve_recv.at[i], device_id=device, device_id_type=MESH,
             ).start()
             return carry
 
         lax.fori_loop(1, 16, body, 0)
         pack(0, me)
-        pltpu.make_async_copy(packed.at[j, 0], recv[j].at[pl.ds(2 * me, 2)], serve_recv.at[j]).start()
-
-    def x_copy(p, j, src_row, dst_row, count, send, rcv, device):
+        pltpu.make_async_copy(packed[i].at[0], recv[i].at[pl.ds(2 * me, 2)], serve_recv.at[i]).start()
+
+    def x_copy(p, i, src, dst, first, count, send, rcv, device):
+        j = PIECES[i][0]
         return pltpu.make_async_remote_copy(
-            src_ref=parts[p].at[j, pl.ds(src_row, count)],
-            dst_ref=parts[p].at[j, pl.ds(dst_row, count)],
-            send_sem=send.at[p, j], recv_sem=rcv.at[p, j], device_id=device, device_id_type=MESH,
+            src_ref=parts[p].at[j, pl.ds(src * quarter(p) + first, count)],
+            dst_ref=parts[p].at[j, pl.ds(dst * quarter(p) + first, count)],
+            send_sem=send.at[p, i], recv_sem=rcv.at[p, i], device_id=device, device_id_type=MESH,
         )
 
     def quarter(p):
         return 2 * rows * len(PARTS[p])
 
-    def hop_right(p, j):
-        return x_copy(p, j, 0, quarter(p), quarter(p), to_right, from_left, right)
-
-    def hop_left(p, j):
-        return x_copy(p, j, 0, 2 * quarter(p), quarter(p), to_left, from_right, left)
-
-    def pass_right(p, j):
-        return x_copy(p, j, quarter(p), 3 * quarter(p), quarter(p) // 2, on_right, opp_left, right)
-
-    def pass_left(p, j):
-        n = quarter(p) // 2
-        return x_copy(p, j, 5 * n, 7 * n, n, on_left, opp_right, left)
-
-    def select_and_send(p, j):
+    def span(p, i):
+        half = PIECES[i][1]
+        return (0, quarter(p)) if half is None else (half * quarter(p) // 2, quarter(p) // 2)
+
+    def hop_right(p, i):
+        return x_copy(p, i, 0, 1, *span(p, i), to_right, from_left, right)
+
+    def hop_left(p, i):
+        return x_copy(p, i, 0, 2, *span(p, i), to_left, from_right, left)
+
+    def pass_right(p, i):
+        first, count = span(p, i)
+        return x_copy(p, i, 1, 3, first, count // 2, on_right, opp_left, right)
+
+    def pass_left(p, i):
+        first, count = span(p, i)
+        return x_copy(p, i, 2, 3, first + count // 2, count // 2, on_left, opp_right, left)
+
+    def select_and_send(p, i):
+        j, half = PIECES[i]
         n = 0
         for g in PARTS[p]:
             for s in (2 * g, 2 * g + 1):
-                parts[p][j, rows * n : rows * n + rows, :] = recv[j][slot_of[s]]
+                one = recv[i][slot_of[s]]
+                for h in (0, 1) if half is None else (half,):
+                    at = h * quarter(p) // 2 + rows // 2 * n
+                    low = rows // 2 * h if half is None else 0
+                    parts[p][j, at : at + rows // 2, :] = one[low : low + rows // 2, :]
                 n += 1
-        hop_right(p, j).start()
-        hop_left(p, j).start()
-
-    def pass_on(p, j):
-        hop_right(p, j).wait_recv()
-        pass_right(p, j).start()
-        hop_left(p, j).wait_recv()
-        pass_left(p, j).start()
+        hop_right(p, i).start()
+        hop_left(p, i).start()
+
+    def pass_on(p, i):
+        hop_right(p, i).wait_recv()
+        pass_right(p, i).start()
+        hop_left(p, i).wait_recv()
+        pass_left(p, i).start()
 
     def project_first(p):
         def body(i, carry):
@@ -242,18 +276,18 @@
     def project_last(p):
         def body(i, carry):
             r = pl.ds(pl.multiple_of(i * quarter(p), quarter(p)), quarter(p))
-            to = pl.ds(pl.multiple_of(i * 2 * rows, 2 * rows), 2 * rows)
             lhs = parts[p][6, r, :]
             k = accs[p][r, 0:512] + jnp.dot(lhs, wk[COL * 6 : COL * 7, :], preferred_element_type=jnp.float32)
             v = accs[p][r, 512:1024] + jnp.dot(lhs, wv[COL * 6 : COL * 7, :], preferred_element_type=jnp.float32)
             k = k.astype(jnp.bfloat16)
             v = v.astype(jnp.bfloat16)
-            for n, g in enumerate(PARTS[p]):
-                keys[g, to, :] = k[2 * rows * n : 2 * rows * (n + 1), :]
-                for m in range(4):
-                    values[g, to, 2 * DH * m : 2 * DH * m + DH] = v[
-                        2 * rows * n : 2 * rows * (n + 1), DH * m : DH * m + DH
-                    ]
+            for h in range(2):
+                to = pl.ds(pl.multiple_of(2 * rows * i + rows * h, rows), rows)
+                for n, g in enumerate(PARTS[p]):
+                    at = h * quarter(p) // 2 + rows * n
+                    keys[g, to, :] = k[at : at + rows, :]
+                    for m in range(4):
+                        values[g, to, 2 * DH * m : 2 * DH * m + DH] = v[at : at + rows, DH * m : DH * m + DH]
             return carry
 
         lax.fori_loop(0, 4, body, 0)
@@ -305,12 +339,12 @@
         pass_right(p, j).wait_recv()
         pass_left(p, j).wait_recv()
         done[p] += 1
-        if done[p] == 6:
+        if done[p] == len(PIECES) - 1:
             if p == 0:
                 loads[2].wait()
                 loads[3].wait()
             project_first(p)
-        if done[p] == 7:
+        if done[p] == len(PIECES):
             project_last(p)
             if p == 0:
                 edge_q.wait_recv()
@@ -324,45 +358,44 @@
                 edge_o.start()
                 write_out((5, 6, 7))
 
-    for j in SERVE[:UPFRONT]:
-        serve(j)
-    served = UPFRONT
+    def drain():
+        edge_q.wait_send()
+        edge_o.wait_send()
+        for i, asked in enumerate((asked_y, asked_z)):
+            pltpu.make_async_copy(asked.at[pl.ds(0, 15)], asked.at[pl.ds(0, 15)], tab_send.at[i]).wait()
+        pltpu.make_async_copy(e_line.at[pl.ds(0, 7)], e_line.at[pl.ds(0, 7)], pre_send.at[0]).wait()
+
+        @pl.when(y != z)
+        def _():
+            spread(0, 1).wait_send()
+
+        for i in SERVE:
+            sent = packed[i].at[pl.ds(1, 15)]
+            pltpu.make_async_copy(sent, sent, serve_send.at[i]).wait()
+        for p, i in UNITS:
+            hop_right(p, i).wait_send()
+            hop_left(p, i).wait_send()
+            pass_right(p, i).wait_send()
+            pass_left(p, i).wait_send()
+        edge_o.wait_recv()
+        wide[0:64, :] = jnp.where(z == 0, 0.0, o_in[...].astype(jnp.float32))
+
     seen = set()
-    for n in range(len(UNITS) + 2 * LOOK):
-        if n < len(UNITS):
-            p, j = UNITS[n]
+    for step in PLAN:
+        if step[0] == "serve":
+            serve(step[1])
+        elif step[0] == "take":
+            p, j = step[1:]
             if j not in seen:
                 seen.add(j)
                 pltpu.make_async_copy(recv[j], recv[j], serve_recv.at[j]).wait()
             select_and_send(p, j)
-            if served < len(SERVE):
-                serve(SERVE[served])
-                served += 1
-        if 0 <= n - LOOK < len(UNITS):
-            pass_on(*UNITS[n - LOOK])
-        if 0 <= n - 2 * LOOK < len(UNITS):
-            if n - 2 * LOOK == len(UNITS) - 1:
-                edge_q.wait_send()
-                edge_o.wait_send()
-                for i, asked in enumerate((asked_y, asked_z)):
-                    pltpu.make_async_copy(asked.at[pl.ds(0, 15)], asked.at[pl.ds(0, 15)], tab_send.at[i]).wait()
-                pltpu.make_async_copy(e_line.at[pl.ds(0, 7)], e_line.at[pl.ds(0, 7)], pre_send.at[0]).wait()
-
-                @pl.when(y != z)
-                def _():
-                    spread(0, 1).wait_send()
-
-                for j in SERVE:
-                    sent = packed.at[j, pl.ds(1, 15)]
-                    pltpu.make_async_copy(sent, sent, serve_send.at[j]).wait()
-                for p, j in UNITS:
-                    hop_right(p, j).wait_send()
-                    hop_left(p, j).wait_send()
-                    pass_right(p, j).wait_send()
-                    pass_left(p, j).wait_send()
-                edge_o.wait_recv()
-                wide[0:64, :] = jnp.where(z == 0, 0.0, o_in[...].astype(jnp.float32))
-            landed(*UNITS[n - 2 * LOOK])
+        elif step[0] == "pass":
+            pass_on(*step[1:])
+        else:
+            if step[1:] == UNITS[-1]:
+                drain()
+            landed(*step[1:])
     write_out((0, 1, 2, 3, 4))
 
 
@@ -370,6 +403,7 @@
     bf16, f32, i32 = jnp.bfloat16, jnp.float32, jnp.int32
     hbm = pl.BlockSpec(memory_space=pl.ANY)
     dma = pltpu.SemaphoreType.DMA
+    piece_rows = [32 if half is None else 16 for _, half in PIECES]
     part_rows = [256 * len(groups) for groups in PARTS]
     return pl.pallas_call(
         exchange_kernel,
@@ -379,7 +413,7 @@
         scratch_shapes=[
             pltpu.VMEM((512, 512), bf16),
             pltpu.VMEM((8, 32, 896), bf16),
-            pltpu.VMEM((8, 32, COL * len(Z_CHUNKS)), bf16),
+            pltpu.VMEM((8, 32, COL * Z_COUNT), bf16),
             pltpu.VMEM((896, 512), bf16),
             pltpu.VMEM((896, 512), bf16),
             pltpu.VMEM((1, 128), i32),
@@ -387,7 +421,6 @@
             pltpu.VMEM((16, 1, 128), i32),
             pltpu.SMEM((16, 1, 128), i32),
             pltpu.SMEM((16, 1, 128), i32),
-            pltpu.VMEM((7, 16, 2, 32, 128), bf16),
             pltpu.VMEM((584, 512), f32),
             pltpu.VMEM((576, 512), bf16),
             pltpu.VMEM((64, 512), bf16),
@@ -395,17 +428,18 @@
             pltpu.VMEM((64, 512), bf16),
             pltpu.VMEM((8, 256, 512), bf16),
             pltpu.VMEM((8, 256, 1024), bf16),
-            pltpu.VMEM((4, 4, 64, 256), f32),
-            pltpu.VMEM((4, 4, 64, 256), bf16),
+            pltpu.VMEM((5, 4, 64, 256), f32),
+            pltpu.VMEM((5, 4, 64, 256), bf16),
         ]
         + [pltpu.VMEM((n, 1024), f32) for n in part_rows]
         + [pltpu.VMEM((7, n, COL), bf16) for n in part_rows]
-        + [pltpu.VMEM((32, 32, 128), bf16) for _ in range(7)]
-        + [dma((4,)), dma((2,)), dma((2,)), dma((2,)), dma((2,)), dma, dma((7,)), dma((7,))]
-        + [dma((len(PARTS), 7)) for _ in range(8)]
+        + [pltpu.VMEM((32, n, COL), bf16) for n in piece_rows]
+        + [pltpu.VMEM((16, 2, n, COL), bf16) for n in piece_rows]
+        + [dma((4,)), dma((2,)), dma((2,)), dma((2,)), dma((2,)), dma, dma((8,)), dma((8,))]
+        + [dma((len(PARTS), 8)) for _ in range(8)]
         + [dma((2,)), dma((2,))],
         compiler_params=pltpu.CompilerParams(
-            collective_id=0, has_side_effects=True, vmem_limit_bytes=60 * 2**20
+            collective_id=0, has_side_effects=True, vmem_limit_bytes=53 * 2**20
         ),
         cost_estimate=pl.CostEstimate(flops=4_100_000_000, bytes_accessed=6_000_000, transcendentals=600_000),
     )(jnp.transpose(neighbour_ids, (0, 2, 1)), queries, encoded, key_weight, value_weight)

time: 74.8 us -> 72.7 us (0.972); the launches traced: 73.4 us -> 72.5 us
    unnamed x1 -> x3, local copies, waits for them, and re-layouts: 1.87 us -> 1.47 us
where the time goes in v3:
time: 72.7 us; the launch traced here: 72.5 us
  Pallas kernels  71 us (98%)
  local copies, waits for them, and re-layouts  1.47 us (2%)
    pallas_call x1, Pallas kernels, local(): pl.pallas_call(exchange_kernel, out_shape=jax.ShapeDtypeStruct(queries.sh...  71 us
    unnamed x3, local copies, waits for them, and re-layouts  1.47 us

profile of v3, /device:TPU:1, one launch (start us, length us, event | category | flops | bytes accessed | tf_op | source)
XLA Modules:
  0.0 72.5 jit_solution(4038436394182333616)
XLA Ops:
  0.0 0.0 copy-start
  0.0 0.7 copy-done
  0.7 71.0 %shard_map.55 = bf16[1,512,512]{2,1,0:T(8,128)(2,1)S(1)} custom-call(s32[1,2,8]{2,1,0:T(2,128)S(1)} %bitcast.1, bf16[1,512,512]{2,1,0:T(8,128)(2,1)} %q_hbm.1, bf16[8,128,896]{2,1,0:T(8,128)(2,1)} %e_hbm.1, bf16[896,512]{1,0:T(8,128)(2,1)} %wk_hbm.1, bf16[896,512]{1,0:T(8,128)(2,1)} %wv_hbm.1), custom_call_target="tpu_custom_call" | custom-call | flops 4100000000 | bytes 6000000 | tf_op jit(solution)/shard_map/pallas_call | solution.py:408
  71.7 0.8 %copy.7 = bf16[1,512,512]{2,1,0:T(8,128)(2,1)} copy(bf16[1,512,512]{2,1,0:T(8,128)(2,1)S(1)} %shard_map.55) | data formatting | bytes 1048576
Async XLA Ops:
  0.0 0.7 copy-start

commit v4 on v3

--- a/solution.py
+++ b/solution.py
@@ -18,6 +18,8 @@
 UNITS = ((0, 0), (1, 0), (0, 1), (1, 1), (0, 5), (0, 2), (1, 5), (0, 6), (0, 3), (0, 7), (1, 2), (0, 4), (1, 6), (1, 3), (1, 7), (1, 4))
 PASS_LAG = 4
 SEE_LAG = 8
+SOON_LAG = 6
+SOON = 11
 
 
 def make_plan():
@@ -27,7 +29,9 @@
             plan.append(("pass",) + UNITS[n - PASS_LAG])
         if n < len(UNITS):
             plan.append(("take",) + UNITS[n])
-        if n >= SEE_LAG:
+        if 0 <= n - SOON_LAG < SOON:
+            plan.append(("see",) + UNITS[n - SOON_LAG])
+        if n - SEE_LAG >= SOON:
             plan.append(("see",) + UNITS[n - SEE_LAG])
     return plan
 

time: 72.7 us -> 72.7 us (level)
  no operation moved by 1% of the time
where the time goes in v4:
time: 72.7 us; the launch traced here: 72.5 us
  Pallas kernels  71 us (98%)
  local copies, waits for them, and re-layouts  1.47 us (2%)
    pallas_call x1, Pallas kernels, local(): pl.pallas_call(exchange_kernel, out_shape=jax.ShapeDtypeStruct(queries.sh...  71 us
    unnamed x3, local copies, waits for them, and re-layouts  1.47 us

profile of v4, /device:TPU:1, one launch (start us, length us, event | category | flops | bytes accessed | tf_op | source)
XLA Modules:
  0.0 72.5 jit_solution(10622938149903296062)
XLA Ops:
  0.0 0.0 copy-start
  0.0 0.7 copy-done
  0.7 71.0 %shard_map.55 = bf16[1,512,512]{2,1,0:T(8,128)(2,1)S(1)} custom-call(s32[1,2,8]{2,1,0:T(2,128)S(1)} %bitcast.1, bf16[1,512,512]{2,1,0:T(8,128)(2,1)} %q_hbm.1, bf16[8,128,896]{2,1,0:T(8,128)(2,1)} %e_hbm.1, bf16[896,512]{1,0:T(8,128)(2,1)} %wk_hbm.1, bf16[896,512]{1,0:T(8,128)(2,1)} %wv_hbm.1), custom_call_target="tpu_custom_call" | custom-call | flops 4100000000 | bytes 6000000 | tf_op jit(solution)/shard_map/pallas_call | solution.py:412
  71.7 0.8 %copy.7 = bf16[1,512,512]{2,1,0:T(8,128)(2,1)} copy(bf16[1,512,512]{2,1,0:T(8,128)(2,1)S(1)} %shard_map.55) | data formatting | bytes 1048576
Async XLA Ops:
  0.0 0.7 copy-start
